TPU v7x, 256 devices: a whole 4x4x8 slice. The times are simulated.
256 devices in a mesh: prow: 8 (over x_lo, y), pcol: 32 (over z, x_hi, core).
Axes of the slice: x: 4 (x_hi: 2, x_lo: 2; x = x_hi * 2 + x_lo), y: 4, z: 8, core: 2. Of those that a mesh axis runs over, the one named last changes fastest.
Arguments:
- panels: bfloat16 [16384, 256], P(('prow', 'pcol')), may hold values from -2 to 42, as said below
- pivots: int32 [2, 128], replicated, may hold values from 0 to 16383, as said below
- trailing: bfloat16 [16384, 32768], P('prow', 'pcol'), may hold values from -6 to 6
Outputs:
- updated: bfloat16 [16384, 32768], P('prow', 'pcol')
- upper_rows: bfloat16 [256, 32768], P(None, 'pcol')
Inputs may be any that keep to these rules, and one draw needn't show every extreme that they name: `pivots`: the 256 pivot rows are distinct; every aligned block of 64 rows holds the same number of them. `panels`: the entry of row pivots[p, i] in column p * 128 + i is 38 or more; every other entry lies within 2 of zero.
All inputs are finite; a program needn't handle non-finite values.
Results may differ from a plain program's by a relative error of at most 0.039.
Values may be sent and summed in bfloat16 or wider, within the bound.
A program may use at most 64 MiB of HBM per device.

v0:
```python
import jax
import jax.numpy as jnp
from jax import lax
from jax.sharding import PartitionSpec as P


def exact_dot(left, right):
    return jnp.dot(left, right, precision=lax.Precision.HIGHEST)


def factor_packed(matrix):
    extent = matrix.shape[0]
    index_all = jnp.arange(extent, dtype=jnp.int32)

    def elimination(pivot_step, current):
        step_now = jnp.asarray(pivot_step).astype(jnp.int32)
        column = lax.dynamic_slice_in_dim(current, step_now, 1, 1)[:, 0]
        pivot_row = lax.dynamic_slice_in_dim(current, step_now, 1, 0)[0]
        pivot_value = lax.dynamic_slice_in_dim(column, step_now, 1, 0)[0]
        below = index_all > step_now
        factor = jnp.where(below, column / pivot_value, jnp.zeros_like(column))
        right_part = jnp.where(below, pivot_row, jnp.zeros_like(pivot_row))
        current = current - factor[:, None] * right_part[None, :]
        place = below[:, None] & (index_all[None, :] == step_now)
        return jnp.where(place, factor[:, None], current)

    return lax.fori_loop(0, extent - 1, elimination, matrix)


def nilpotent_inverse(strict):
    extent = strict.shape[0]
    identity = jnp.eye(extent, dtype=jnp.float32)
    powered = strict
    result = identity - strict
    for _ in range((extent - 1).bit_length() - 1):
        powered = exact_dot(powered, powered)
        result = exact_dot(result, identity + powered)
    return result


def triangular_inverses(packed):
    diagonal = jnp.diagonal(packed)
    inv_lower = nilpotent_inverse(jnp.tril(packed, -1))
    inv_upper = nilpotent_inverse(jnp.triu(packed, 1) / diagonal[:, None]) / diagonal[None, :]
    return (inv_lower, inv_upper)


def pivot_factors(picked):
    panel_width = picked.shape[0] // 2
    inv_lower_one, inv_upper_one = triangular_inverses(
        factor_packed(picked[:panel_width, :panel_width])
    )
    cross_upper = exact_dot(inv_lower_one, picked[:panel_width, panel_width:]).astype(jnp.bfloat16)
    left_pivots = exact_dot(picked[panel_width:, :panel_width], inv_upper_one).astype(jnp.bfloat16)
    second_block = picked[panel_width:, panel_width:] - jnp.dot(
        left_pivots, cross_upper, preferred_element_type=jnp.float32
    )
    inv_lower_two, inv_upper_two = triangular_inverses(factor_packed(second_block))
    return (inv_lower_one, inv_upper_one, cross_upper, left_pivots, inv_lower_two, inv_upper_two)


def panel_rows(raw_rows, inv_upper_one, cross_upper, inv_upper_two):
    panel_width = cross_upper.shape[0]
    lower_one = exact_dot(raw_rows[:, :panel_width].astype(jnp.float32), inv_upper_one).astype(
        jnp.bfloat16
    )
    second_cols = raw_rows[:, panel_width:].astype(jnp.float32) - jnp.dot(
        lower_one, cross_upper, preferred_element_type=jnp.float32
    )
    lower_two = exact_dot(second_cols, inv_upper_two).astype(jnp.bfloat16)
    return jnp.concatenate([lower_one, lower_two], axis=1)


def upper_solve(chosen, inv_lower_one, left_pivots, inv_lower_two):
    panel_width = left_pivots.shape[0]
    upper_one = exact_dot(inv_lower_one, chosen[:panel_width]).astype(jnp.bfloat16)
    inner = chosen[panel_width:] - jnp.dot(
        left_pivots, upper_one, preferred_element_type=jnp.float32
    )
    upper_two = exact_dot(inv_lower_two, inner).astype(jnp.bfloat16)
    return jnp.concatenate([upper_one, upper_two], axis=0)


def local_pick(source, wanted, row_base):
    local_ids = wanted - row_base
    inside = (local_ids >= 0) & (local_ids < source.shape[0])
    clipped = jnp.clip(local_ids, 0, source.shape[0] - 1)
    return jnp.where(inside[:, None], jnp.take(source, clipped, axis=0).astype(jnp.float32), 0.0)


def local(panels, pivots, trailing):
    rows_dev = panels.shape[0]
    prow_rows = trailing.shape[0]
    flat_piv = pivots.reshape(-1)
    device_id = lax.axis_index("prow") * lax.axis_size("pcol") + lax.axis_index("pcol")
    device_base = device_id * rows_dev
    picked = lax.psum(local_pick(panels, flat_piv, device_base), ("prow", "pcol"))
    prow_base = lax.axis_index("prow") * prow_rows
    chosen = lax.psum(
        local_pick(trailing, flat_piv, prow_base).astype(jnp.bfloat16), "prow"
    ).astype(jnp.float32)
    inv_lower_one, inv_upper_one, cross_upper, left_pivots, inv_lower_two, inv_upper_two = (
        pivot_factors(picked)
    )
    upper_rows = upper_solve(chosen, inv_lower_one, left_pivots, inv_lower_two)
    own_factors = panel_rows(panels, inv_upper_one, cross_upper, inv_upper_two)
    updated = (
        trailing.astype(jnp.float32)
        - jnp.dot(
            lax.all_gather(own_factors, "pcol", axis=0, tiled=True),
            upper_rows,
            preferred_element_type=jnp.float32,
        )
    ).astype(jnp.bfloat16)
    return (updated, upper_rows)


def solution(mesh):
    return jax.shard_map(
        local,
        mesh=mesh,
        in_specs=(P(("prow", "pcol"), None), P(), P("prow", "pcol")),
        out_specs=(P("prow", "pcol"), P(None, "pcol")),
        check_vma=False,
    )
```

profile of v0, /device:TPU:1, one launch (start us, length us, event | category | flops | bytes accessed | tf_op | source)
XLA Modules:
  0.0 755.5 jit_solution(1054105669306312287)
XLA Ops:
  7.2 0.7 and_bitcast_fusion
  7.9 0.7 compare_and_fusion
  8.6 1.7 gather_fusion
  10.3 0.8 convert_select_fusion
  11.3 4.3 gather_fusion.3
  15.6 1.0 select_convert_fusion
  16.9 249.7 %all-reduce.3.cloned.1.call-done = f32[256,256]{1,0:T(8,128)} async-done(((f32[256,256]{1,0:T(8,128)}), f32[256,256]{1,0:T(8,128)}) %all-reduce.3.cloned.1.call-update) | async-done | bytes 262160 | tf_op jit(solution)/shard_map/psum | solution.py:97
  266.6 0.9 slice.44
  267.6 191.6 %while.36 = (s32[]{:T(128)}, f32[128,128]{0,1:T(8,128)S(1)}, s32[]{:T(128)}, s32[]{:T(128)}, s32[]{:T(128)}) while((s32[]{:T(128)}, f32[128,128]{0,1:T(8,128)S(1)}, s32[]{:T(128)}, s32[]{:T(128)}, s32[]{:T(128)}) %tuple.104), condition=%wide.region_2.3_spmd.clone.clone, body=%wide.region_1.2_spmd.clone.clone.sunk | while | flops 66435 | bytes 267881 | solution.py:27
  268.2 0.7 fusion.161
  271.3 0.7 fusion.161
  281.8 0.7 fusion.161
  286.4 0.7 fusion.161
  287.9 0.7 fusion.161
  292.4 0.7 fusion.161
  295.4 0.7 fusion.161
  298.4 0.7 fusion.161
  299.9 0.7 fusion.161
  301.4 0.7 fusion.161
  304.5 0.7 fusion.161
  319.6 0.7 fusion.161
  321.1 0.7 fusion.161
  322.6 0.7 fusion.161
  331.6 0.7 fusion.161
  333.1 0.7 fusion.161
  459.4 1.3 gather_fusion.1
  466.9 191.7 %while.37 = (s32[]{:T(128)}, f32[128,128]{0,1:T(8,128)S(1)}, s32[]{:T(128)}, s32[]{:T(128)}, s32[]{:T(128)}) while((s32[]{:T(128)}, f32[128,128]{0,1:T(8,128)S(1)}, s32[]{:T(128)}, s32[]{:T(128)}, s32[]{:T(128)}) %tuple.107), condition=%wide.region_4.5_spmd.clone.clone, body=%wide.region_3.4_spmd.clone.clone.sunk | while | flops 66435 | bytes 267881 | solution.py:27
  658.6 1.3 gather_fusion.2
  666.4 1.3 convolution_convert_fusion.1
  667.7 1.2 convolution_subtract_fusion
  669.5 73.7 %all-gather.2.cloned.1.call-done = bf16[2048,256]{1,0:T(8,128)(2,1)} async-done(((bf16[64,256]{1,0:T(8,128)(2,1)}), bf16[2048,256]{1,0:T(8,128)(2,1)}) %all-gather.2.cloned.1.call-update) | async-done | bytes 1048592 | tf_op jit(solution)/shard_map/all_gather | solution.py:110
  743.2 5.8 subtract_convert_fusion
  (1588 shorter events, 372.7 us)
Async XLA Ops:
  7.2 259.5 %all-reduce.3.cloned.1.call-start = ((), (), s32[]{:S(2)}) async-start(), calls=%async_computation | async-start | bytes 524288 | tf_op jit(solution)/shard_map/psum | solution.py:97
  11.2 655.1 %all-reduce.5.cloned.1.call-start = ((), (), s32[]{:S(2)}) async-start(), calls=%async_computation.2 | async-start | bytes 1048576 | tf_op jit(solution)/shard_map/psum | solution.py:99
  15.6 448.6 %copy-start = (bf16[64,256]{1,0:T(8,128)(2,1)S(1)}, bf16[64,256]{1,0:T(8,128)(2,1)}, u32[]{:S(2)}) copy-start(bf16[64,256]{1,0:T(8,128)(2,1)} %param.7) | copy-start | bytes 98308
  16.6 726.6 %all-gather.2.cloned.1.call-start = ((), (), s32[]{:S(2)}) async-start(), calls=%async_computation.1 | async-start | bytes 1081344 | tf_op jit(solution)/shard_map/all_gather | solution.py:110
  266.6 199.6 %copy-start.2 = (f32[256,256]{1,0:T(8,128)S(1)}, f32[256,256]{1,0:T(8,128)}, u32[]{:S(2)}) copy-start(f32[256,256]{1,0:T(8,128)} %all-reduce.3.cloned.1.call-done) | copy-start | bytes 786436
  669.5 79.5 %copy-start.1 = (bf16[256,1024]{1,0:T(8,128)(2,1)}, bf16[256,1024]{1,0:T(8,128)(2,1)S(1)}, u32[]{:S(2)}) copy-start(bf16[256,1024]{1,0:T(8,128)(2,1)S(1)} %pad_maximum_fusion) | copy-start | bytes 1572868
Sparse Core Ops, SparseCore 0:
  14.0 252.5 all-reduce.2
  269.8 75.1 all-reduce.4
  665.2 78.0 all-gather.1
where the time goes:
time: 758 us; the launch traced here: 756 us
  waiting for transfers between devices  324 us (43%)
  other arithmetic  202 us (27%)
  local copies, waits for them, and re-layouts  182 us (24%)
  matrix products  20.2 us (3%)
  between operations  14.3 us (2%)
  loops' own time  13.6 us (2%)
    psum x1, waiting for transfers between devices, local(): lax.psum(local_pick(panels, flat_piv, device_base), ('prow', 'pcol'))  250 us
    broadcast_in_dim x254, other arithmetic, elimination(): return jnp.where(place, factor[:, None], current)  166 us
    dynamic_slice x254, local copies, waits for them, and re-layouts, elimination(): pivot_value = lax.dynamic_slice_in_dim(column, step_now, 1, 0)[0]  149 us
    all_gather x1, waiting for transfers between devices, local(): lax.all_gather(own_factors, 'pcol', axis=0, tiled=True)  73.7 us
    select_n x254, other arithmetic, elimination(): return jnp.where(place, factor[:, None], current)  27 us
    while x254, local copies, waits for them, and re-layouts  22.3 us
  transfers between devices with their start and end apart: 3, of which 2 were waited for; matrix products, arithmetic and copies ran while one was open for 52% of the time, Pallas kernels for 0%

commit v1 on v0

v1 whole, which is shorter than its diff:
```python
import functools

import jax
import jax.numpy as jnp
from jax import lax
from jax.experimental import pallas as pl
from jax.experimental.pallas import tpu as pltpu
from jax.sharding import PartitionSpec as P

f32, bf16, i32 = jnp.float32, jnp.bfloat16, jnp.int32
MESH = pl.DeviceIdType.MESH
T_PARTS = 4
OUT_PARTS = 8


def split(x):
    high = x.astype(bf16)
    return high, (x - high.astype(f32)).astype(bf16)


def gather_kernel(
    n_prow, n_pcol, pivots, panels, trailing, g_out, c_out, p_out, t_buf, rows_buf,
    t_sem, s1_send, s1_recv, z_send, z_recv, x_send, x_recv, sib_send, sib_recv,
    g_send, g_recv, c_send, c_recv,
):
    n_z = n_pcol // 4
    prow, pcol = lax.axis_index("prow"), lax.axis_index("pcol")
    z, place = pcol // 4, lax.rem(pcol, 4)
    x_hi, core = place // 2, lax.rem(place, 2)
    rows_dev = panels.shape[0]
    part_rows = trailing.shape[0] // T_PARTS

    def t_copy(q):
        at = pl.ds(q * part_rows, part_rows)
        return pltpu.make_async_copy(trailing.at[at], t_buf.at[at], t_sem.at[q])

    for q in range(T_PARTS):
        t_copy(q).start()

    barrier = pltpu.get_barrier_semaphore()

    @pl.loop(1, n_pcol)
    def _(step):
        pl.semaphore_signal(
            barrier, inc=1, device_id={"pcol": lax.rem(pcol + step, n_pcol)}, device_id_type=MESH
        )

    @pl.loop(1, n_prow)
    def _(step):
        pl.semaphore_signal(
            barrier, inc=1, device_id={"prow": lax.rem(prow + step, n_prow)}, device_id_type=MESH
        )

    block = pivots[...] // rows_dev
    offset = pivots[...] - block * rows_dev
    offset_f = offset.astype(f32)
    own = jnp.where(block == prow * n_pcol + pcol, offset_f, 0.0)
    own_offset = jnp.sum(jnp.sum(own, axis=0, keepdims=True), axis=1, keepdims=True)
    lane = lax.broadcasted_iota(i32, (16, rows_dev), 1).astype(f32)
    pick = jnp.where(lane == own_offset, 1.0, 0.0).astype(bf16)
    own_row = jnp.dot(pick, panels[...], preferred_element_type=f32)
    rows_buf[pcol] = own_row[0:1, :]
    p_out[z, place] = panels[...]
    sub = lax.broadcasted_iota(i32, (n_pcol, pivots.shape[1]), 0) + prow * n_pcol
    found = jnp.where(block[0:1, :] == sub, offset_f[0:1, :], 0.0) + jnp.where(
        block[1:2, :] == sub, offset_f[1:2, :], 0.0
    )
    row_at = jnp.sum(found, axis=1, keepdims=True) + (
        lax.broadcasted_iota(i32, (n_pcol, 1), 0) * rows_dev
    ).astype(f32)

    pl.semaphore_wait(barrier, n_pcol - 1 + n_prow - 1)

    def s1_copy(source, target):
        return pltpu.make_async_remote_copy(
            src_ref=rows_buf.at[source], dst_ref=rows_buf.at[source],
            send_sem=s1_send.at[target], recv_sem=s1_recv.at[source],
            device_id={"pcol": target}, device_id_type=MESH,
        )

    @pl.loop(1, n_pcol)
    def _(step):
        s1_copy(pcol, lax.rem(pcol + step, n_pcol)).start()

    def z_copy(source, target):
        return pltpu.make_async_remote_copy(
            src_ref=p_out.at[source, place], dst_ref=p_out.at[source, place],
            send_sem=z_send.at[target], recv_sem=z_recv.at[source],
            device_id={"pcol": target * 4 + place}, device_id_type=MESH,
        )

    def x_copy(at_z, at_place):
        return pltpu.make_async_remote_copy(
            src_ref=p_out.at[at_z, at_place], dst_ref=p_out.at[at_z, at_place],
            send_sem=x_send.at[at_z], recv_sem=x_recv.at[at_z],
            device_id={"pcol": z * 4 + (1 - x_hi) * 2 + core}, device_id_type=MESH,
        )

    def sib_copy(slot, at_place):
        return pltpu.make_async_remote_copy(
            src_ref=p_out.at[:, at_place], dst_ref=p_out.at[:, at_place],
            send_sem=sib_send.at[slot], recv_sem=sib_recv.at[slot],
            device_id={"pcol": z * 4 + x_hi * 2 + (1 - core)}, device_id_type=MESH,
        )

    def z_at(step):
        half = (step + 1) // 2
        return lax.rem(z + n_z + jnp.where(lax.rem(step, 2) == 1, half, -half), n_z)

    @pl.loop(1, n_z)
    def _(step):
        z_copy(z, z_at(step)).start()

    x_copy(z, place).start()

    chosen = jnp.zeros((n_pcol, trailing.shape[1]), f32)
    for q in range(T_PARTS):
        t_copy(q).wait()
        lane = lax.broadcasted_iota(i32, (n_pcol, part_rows), 1).astype(f32) + q * part_rows
        pick = jnp.where(lane == row_at, 1.0, 0.0).astype(bf16)
        chosen = chosen + jnp.dot(
            pick, t_buf[q * part_rows:(q + 1) * part_rows, :], preferred_element_type=f32
        )
    own_rows = pl.ds(pl.multiple_of(prow * n_pcol, n_pcol), n_pcol)
    c_out[own_rows, :] = chosen.astype(bf16)

    def down_copy(ref, send, recv, source, target):
        at = pl.ds(pl.multiple_of(source * n_pcol, n_pcol), n_pcol)
        return pltpu.make_async_remote_copy(
            src_ref=ref.at[at], dst_ref=ref.at[at],
            send_sem=send.at[target], recv_sem=recv.at[source],
            device_id={"prow": target}, device_id_type=MESH,
        )

    g_copy = functools.partial(down_copy, g_out, g_send, g_recv)
    c_copy = functools.partial(down_copy, c_out, c_send, c_recv)

    @pl.loop(1, n_pcol)
    def _(step):
        s1_copy(lax.rem(pcol + step, n_pcol), pcol).wait_recv()

    g_out[own_rows, :] = rows_buf[:, 0, :].astype(bf16)

    @pl.loop(1, n_prow)
    def _(step):
        g_copy(prow, lax.rem(prow + step, n_prow)).start()

    @pl.loop(1, n_prow)
    def _(step):
        c_copy(prow, lax.rem(prow + step, n_prow)).start()

    @pl.loop(1, n_z)
    def _(step):
        from_z = z_at(step)
        z_copy(from_z, z).wait_recv()
        x_copy(from_z, place).start()

    sib_copy(0, place).start()
    other = (1 - x_hi) * 2 + core

    @pl.loop(0, n_z)
    def _(step):
        x_copy(z_at(step), other).wait_recv()

    sib_copy(1, other).start()

    @pl.loop(1, n_prow)
    def _(step):
        g_copy(lax.rem(prow + step, n_prow), prow).wait_recv()

    @pl.loop(1, n_prow)
    def _(step):
        c_copy(lax.rem(prow + step, n_prow), prow).wait_recv()

    sib_copy(0, x_hi * 2 + 1 - core).wait_recv()
    sib_copy(1, (1 - x_hi) * 2 + 1 - core).wait_recv()

    @pl.loop(1, n_pcol)
    def _(step):
        s1_copy(pcol, lax.rem(pcol + step, n_pcol)).wait_send()

    @pl.loop(1, n_z)
    def _(step):
        z_copy(z, z_at(step)).wait_send()

    @pl.loop(0, n_z)
    def _(step):
        x_copy(z_at(step), place).wait_send()

    sib_copy(0, place).wait_send()
    sib_copy(1, other).wait_send()

    @pl.loop(1, n_prow)
    def _(step):
        g_copy(prow, lax.rem(prow + step, n_prow)).wait_send()
        c_copy(prow, lax.rem(prow + step, n_prow)).wait_send()


def gather_all(n_prow, n_pcol, pivots, panels, trailing):
    rows_dev, width = panels.shape
    n_dev, n_z = n_prow * n_pcol, n_pcol // 4
    dma = pltpu.SemaphoreType.DMA
    vmem = pl.BlockSpec(memory_space=pltpu.VMEM)
    return pl.pallas_call(
        functools.partial(gather_kernel, n_prow, n_pcol),
        out_shape=[
            jax.ShapeDtypeStruct((n_dev, width), bf16),
            jax.ShapeDtypeStruct((n_dev, trailing.shape[1]), bf16),
            jax.ShapeDtypeStruct((n_z, 4, rows_dev, width), bf16),
        ],
        in_specs=[vmem, vmem, pl.BlockSpec(memory_space=pl.ANY)],
        out_specs=[vmem] * 3,
        scratch_shapes=[
            pltpu.VMEM(trailing.shape, bf16),
            pltpu.VMEM((n_pcol, 1, width), f32),
            dma((T_PARTS,)),
            dma((n_pcol,)), dma((n_pcol,)),
            dma((n_z,)), dma((n_z,)), dma((n_z,)), dma((n_z,)),
            dma((2,)), dma((2,)),
            dma((n_prow,)), dma((n_prow,)), dma((n_prow,)), dma((n_prow,)),
        ],
        compiler_params=pltpu.CompilerParams(
            collective_id=0, has_side_effects=True, vmem_limit_bytes=32 * 1024 * 1024
        ),
        name="gather_rows",
    )(pivots, panels, trailing)


def block_elimination(rows, first, extent):
    sub = lax.broadcasted_iota(i32, (extent, 128), 0)
    piece, lane = divmod(first, 128)

    def across(x, k):
        return jnp.broadcast_to(x[k:k + 1, :], (extent, 128))

    columns = [
        jnp.broadcast_to(rows[piece][:, lane + k:lane + k + 1], (extent, 128))
        for k in range(extent)
    ]
    upper = []
    inverse = jnp.zeros((extent, 128), f32)
    for k in range(extent):
        reciprocal = 1.0 / across(columns[k], k)
        factor = jnp.where(sub == k, 0.0, columns[k] * reciprocal)
        inverse = jnp.where(sub == k, reciprocal, inverse)
        upper.append([x[k:k + 1, :] for x in rows[2:]])
        for later in range(k + 1, extent):
            columns[later] = columns[later] - factor * across(columns[later], k)
        rows = [x - factor * across(x, k) for x in rows]
    return [x * inverse for x in rows], upper


def eliminate(work, rhs, lower_inv, extent):
    rhs[...] = jnp.zeros_like(rhs)
    for first in range(0, 256, extent):
        piece, lane = divmod(first, 128)
        block = slice(first, first + extent)
        rows = [work[block, 128 * q:128 * q + 128] for q in range(4)]
        rows, upper = block_elimination(rows, first, extent)
        for k in range(extent):
            for q in range(2):
                lower_inv[first + k:first + k + 1, 128 * q:128 * q + 128] = upper[k][q]
        high, low = split(work[:, 128 * piece:128 * piece + 128])
        left = jnp.concatenate([high, low], axis=1)
        live = [q for q in range(4) if (q + 1) * 128 > first]
        at = (slice(lane, lane + extent), slice(128 + lane, 128 + lane + extent))
        for q in live:
            for part, value in enumerate(split(rows[q])):
                for place in at:
                    rhs[part, place, 128 * q:128 * q + 128] = value
        for half in range(2):
            if half == 0 and first + extent >= 256:
                continue
            columns = slice(256 * half, 256 * half + 256)
            work[:, columns] = work[:, columns] - (
                jnp.dot(left, rhs[0, :, columns], preferred_element_type=f32)
                + jnp.dot(left, rhs[1, :, columns], preferred_element_type=f32)
            )
        for q in live:
            work[block, 128 * q:128 * q + 128] = rows[q]
            for part in range(2):
                for place in at:
                    rhs[part, place, 128 * q:128 * q + 128] = jnp.zeros((extent, 128), bf16)


def solve_kernel(
    rows_dev, pivots, gathered, chosen, panels, trailing, updated, upper_rows,
    work, rhs, lower_inv, t_buf, p_buf, c_buf, x_buf, t_sem, o_sem, p_sem, c_sem,
):
    part_rows = trailing.shape[0] // OUT_PARTS

    def t_copy(q):
        at = pl.ds(q * part_rows, part_rows)
        return pltpu.make_async_copy(trailing.at[at], t_buf.at[at], t_sem.at[q])

    def o_copy(q):
        at = pl.ds(q * part_rows, part_rows)
        return pltpu.make_async_copy(t_buf.at[at], updated.at[at], o_sem.at[q])

    c_copy = pltpu.make_async_copy(chosen, c_buf, c_sem)
    p_copy = pltpu.make_async_copy(panels, p_buf, p_sem)
    c_copy.start()
    p_copy.start()
    for q in range(OUT_PARTS):
        t_copy(q).start()

    block = (pivots[...] // rows_dev).astype(f32)
    for half in range(2):
        turned = jnp.transpose(jnp.broadcast_to(block[half:half + 1, :], (128, 128)))
        for q in range(2):
            lane = lax.broadcasted_iota(i32, (128, 128), 1).astype(f32) + 128 * q
            work[128 * half:128 * half + 128, 256 + 128 * q:384 + 128 * q] = jnp.where(
                turned == lane, 1.0, 0.0
            )
    work[:, :256] = jnp.dot(
        work[:, 256:].astype(bf16), gathered[...], preferred_element_type=f32
    )
    eliminate(work, rhs, lower_inv, 16)

    def product(left, right):
        high, low = split(left)
        return jnp.dot(high, right, preferred_element_type=f32) + jnp.dot(
            low, right, preferred_element_type=f32
        )

    c_copy.wait()
    x_buf[...] = product(work[:, 256:], c_buf[...]).astype(bf16)
    upper_rows[...] = product(lower_inv[...], c_buf[...]).astype(bf16)
    p_copy.wait()
    for q in range(OUT_PARTS):
        t_copy(q).wait()
        at = slice(q * part_rows, (q + 1) * part_rows)
        t_buf[at, :] = (
            t_buf[at, :].astype(f32)
            - jnp.dot(p_buf[at, :], x_buf[...], preferred_element_type=f32)
        ).astype(bf16)
        o_copy(q).start()
    for q in range(OUT_PARTS):
        o_copy(q).wait()


def solve(pivots, gathered, chosen, panels, trailing, rows_dev):
    width, columns = chosen.shape
    dma = pltpu.SemaphoreType.DMA
    vmem, anywhere = pl.BlockSpec(memory_space=pltpu.VMEM), pl.BlockSpec(memory_space=pl.ANY)
    return pl.pallas_call(
        functools.partial(solve_kernel, rows_dev),
        out_shape=[
            jax.ShapeDtypeStruct(trailing.shape, bf16),
            jax.ShapeDtypeStruct((width, columns), bf16),
        ],
        in_specs=[vmem, vmem, anywhere, anywhere, anywhere],
        out_specs=[anywhere, vmem],
        scratch_shapes=[
            pltpu.VMEM((width, 2 * width), f32),
            pltpu.VMEM((2, width, 2 * width), bf16),
            pltpu.VMEM((width, width), f32),
            pltpu.VMEM(trailing.shape, bf16),
            pltpu.VMEM(panels.shape, bf16),
            pltpu.VMEM((width, columns), bf16),
            pltpu.VMEM((width, columns), bf16),
            dma((OUT_PARTS,)), dma((OUT_PARTS,)), dma(()), dma(()),
        ],
        compiler_params=pltpu.CompilerParams(vmem_limit_bytes=40 * 1024 * 1024),
        name="solve_update",
    )(pivots, gathered, chosen, panels, trailing)


def solution(mesh):
    n_prow, n_pcol = mesh.shape["prow"], mesh.shape["pcol"]

    def local(panels, pivots, trailing):
        gathered, chosen, rows = gather_all(n_prow, n_pcol, pivots, panels, trailing)
        rows = rows.reshape(trailing.shape[0], panels.shape[1])
        updated, upper_rows = solve(pivots, gathered, chosen, rows, trailing, panels.shape[0])
        return updated, upper_rows

    return jax.shard_map(
        local,
        mesh=mesh,
        in_specs=(P(("prow", "pcol"), None), P(), P("prow", "pcol")),
        out_specs=(P("prow", "pcol"), P(None, "pcol")),
        check_vma=False,
    )
```

time: 758 us -> 53.8 us (0.07)
  waiting for transfers between devices: 324 us -> 0 us
  other arithmetic: 202 us -> 0 us
  local copies, waits for them, and re-layouts: 182 us -> 3.62 us
  Pallas kernels: 0 us -> 49.3 us
  matrix products: 20.2 us -> 0 us
  between operations: 14.3 us -> 0.67 us
  loops' own time: 13.6 us -> 0 us
    psum x2 -> x0, waiting for transfers between devices: 250 us -> none  [the longest x1 250 us: local(): lax.psum(local_pick(panels, flat_piv, device_base), ('prow', 'pcol'))]
    broadcast_in_dim x254 -> x0, other arithmetic: 166 us -> none  [elimination(): return jnp.where(place, factor[:, None], current)]
    dynamic_slice x254 -> x0, local copies, waits for them, and re-layouts: 149 us -> none  [elimination(): pivot_value = lax.dynamic_slice_in_dim(column, step_now, 1, 0)[0]]
    all_gather x1 -> x0, waiting for transfers between devices: 73.7 us -> none  [local(): lax.all_gather(own_factors, 'pcol', axis=0, tiled=True)]
    pallas_call x0 -> x2, Pallas kernels: none -> 49.3 us  [the longest x1 34.5 us: gather_all(): pl.pallas_call(functools.partial(gather_kernel, n_prow, n_pcol), out_shap...]
    select_n x257 -> x0, other arithmetic: 27.9 us -> none  [the longest x254 27 us: elimination(): return jnp.where(place, factor[:, None], current)]
    while x256 -> x0, local copies, waits for them, and re-layouts: 22.5 us -> none
    dot_general x58 -> x0, matrix products: 20.2 us -> none  [the longest x54 13 us: exact_dot(): return jnp.dot(left, right, precision=lax.Precision.HIGHEST)]
  transfers between devices with their start and end apart: 3 -> 0, of which waited for: 2 -> 0; matrix products, arithmetic and copies ran while one was open for 52% -> 0% of each run, Pallas kernels for 0% -> 0%
where the time goes in v1:
time: 53.8 us; the launch traced here: 53.6 us
  Pallas kernels  49.3 us (92%)
  local copies, waits for them, and re-layouts  3.62 us (7%)
  between operations  0.67 us (1%)
    pallas_call x1, Pallas kernels, gather_all(): pl.pallas_call(functools.partial(gather_kernel, n_prow, n_pcol), out_shap...  34.5 us
    pallas_call x1, Pallas kernels, solve(): pl.pallas_call(functools.partial(solve_kernel, rows_dev), out_shape=[jax....  14.8 us
    unnamed x10, local copies, waits for them, and re-layouts  3.62 us

profile of v1, /device:TPU:1, one launch (start us, length us, event | category | flops | bytes accessed | tf_op | source)
XLA Modules:
  0.0 53.6 jit_solution(1788798879483492465)
XLA Ops:
  0.6 0.0 copy-start
  0.6 2.2 %copy-done = bf16[2048,1024]{1,0:T(8,128)(2,1)S(1)} copy-done((bf16[2048,1024]{1,0:T(8,128)(2,1)S(1)}, bf16[2048,1024]{1,0:T(8,128)(2,1)}, u32[]{:S(2)}) %copy-start) | copy-done | bytes 4194328
  2.8 0.0 copy-start.2
  2.8 0.8 %copy-done.2 = bf16[64,256]{1,0:T(8,128)(2,1)S(1)} copy-done((bf16[64,256]{1,0:T(8,128)(2,1)S(1)}, bf16[64,256]{1,0:T(8,128)(2,1)}, u32[]{:S(2)}) %copy-start.2) | copy-done | bytes 32792
  3.6 0.0 copy-start.3
  3.6 0.7 %copy-done.3 = s32[2,128]{1,0:T(2,128)S(1)} copy-done((s32[2,128]{1,0:T(2,128)S(1)}, s32[2,128]{1,0:T(2,128)}, u32[]{:S(2)}) %copy-start.3) | copy-done | bytes 1048
  4.3 0.0 copy-start.1
  4.3 0.0 copy-start.4
  4.3 34.5 %gather_rows.1 = (bf16[256,256]{1,0:T(8,128)(2,1)S(1)}, bf16[256,1024]{1,0:T(8,128)(2,1)S(1)}, bf16[8,4,64,256]{3,2,1,0:T(8,128)(2,1)S(1)}) custom-call(s32[2,128]{1,0:T(2,128)S(1)} %copy-done.3, bf16[64,256]{1,0:T(8,128)(2,1)S(1)} %copy-done.2, bf16[2048,1024]{1,0:T(8,128)(2,1)S(1)} %copy-done), custom_call_target="tpu_custom_call" | custom-call | tf_op jit(solution)/shard_map/gather_rows/pallas_call | solution.py:204
  38.8 0.0 copy-done.1
  38.8 0.0 copy-done.4
  38.8 14.8 %solve_update.1 = (bf16[2048,1024]{1,0:T(8,128)(2,1)}, bf16[256,1024]{1,0:T(8,128)(2,1)}) custom-call(s32[2,128]{1,0:T(2,128)S(1)} %copy-done.4, bf16[256,256]{1,0:T(8,128)(2,1)S(1)} %get-tuple-element.5.gathered, bf16[256,1024]{1,0:T(8,128)(2,1)S(1)} %get-tuple-element.6.chosen, bf16[2048,256]{1,0:T(8,128)(2,1)S(1)} %bitcast.1, bf16[2048,1024]{1,0:T(8,128)(2,1)S(1)} %copy-done.1), custom_call_target="tpu_custom_call" | custom-call | tf_op jit(solution)/shard_map/solve_update/pallas_call | solution.py:346
Async XLA Ops:
  0.6 2.2 %copy-start = (bf16[2048,1024]{1,0:T(8,128)(2,1)S(1)}, bf16[2048,1024]{1,0:T(8,128)(2,1)}, u32[]{:S(2)}) copy-start(bf16[2048,1024]{1,0:T(8,128)(2,1)} %trailing.3) | copy-start | bytes 12582916
  2.8 0.8 %copy-start.2 = (bf16[64,256]{1,0:T(8,128)(2,1)S(1)}, bf16[64,256]{1,0:T(8,128)(2,1)}, u32[]{:S(2)}) copy-start(bf16[64,256]{1,0:T(8,128)(2,1)} %panels.1) | copy-start | bytes 98308
  3.6 0.7 %copy-start.3 = (s32[2,128]{1,0:T(2,128)S(1)}, s32[2,128]{1,0:T(2,128)}, u32[]{:S(2)}) copy-start(s32[2,128]{1,0:T(2,128)} %pivots.3) | copy-start | bytes 3076
  4.3 34.5 %copy-start.1 = (bf16[2048,1024]{1,0:T(8,128)(2,1)S(1)}, bf16[2048,1024]{1,0:T(8,128)(2,1)}, u32[]{:S(2)}) copy-start(bf16[2048,1024]{1,0:T(8,128)(2,1)} %trailing.3) | copy-start | bytes 12582916
  4.3 34.5 %copy-start.4 = (s32[2,128]{1,0:T(2,128)S(1)}, s32[2,128]{1,0:T(2,128)}, u32[]{:S(2)}) copy-start(s32[2,128]{1,0:T(2,128)} %pivots.3) | copy-start | bytes 3076

commit v2 on v1

v2 whole, which is shorter than its diff:
```python
import functools

import jax
import jax.numpy as jnp
from jax import lax
from jax.experimental import pallas as pl
from jax.experimental.pallas import tpu as pltpu
from jax.sharding import PartitionSpec as P

f32, bf16, i32 = jnp.float32, jnp.bfloat16, jnp.int32
MESH = pl.DeviceIdType.MESH
T_PARTS = 4
OUT_PARTS = 8


def split(x):
    high = x.astype(bf16)
    return high, (x - high.astype(f32)).astype(bf16)


def factor_kernel(
    n_prow, n_pcol, pivots, panels, trailing, lower_inv, full_inv, c_out, p_out,
    t_buf, piv_buf, z_rows, q_rows, y_rows, work, order, rhs,
    t_sem, in_sem, a_send, a_recv, z_send, z_recv, x_send, x_recv, sib_send, sib_recv,
    c_send, c_recv,
):
    n_z, n_y = n_pcol // 4, n_prow // 2
    prow, pcol = lax.axis_index("prow"), lax.axis_index("pcol")
    x_lo, y = prow // n_y, lax.rem(prow, n_y)
    z, place = pcol // 4, lax.rem(pcol, 4)
    x_hi, core = place // 2, lax.rem(place, 2)
    q = x_lo * 4 + place
    rows_dev = panels.shape[0]
    part_rows = trailing.shape[0] // T_PARTS

    def t_copy(part):
        at = pl.ds(part * part_rows, part_rows)
        return pltpu.make_async_copy(trailing.at[at], t_buf.at[at], t_sem.at[part])

    piv_copy = pltpu.make_async_copy(pivots, piv_buf, in_sem.at[0])
    own_copy = pltpu.make_async_copy(panels, p_out.at[z, place], in_sem.at[1])
    piv_copy.start()
    own_copy.start()
    for part in range(T_PARTS):
        t_copy(part).start()

    def z_peer(step):
        at = lax.rem(z + step, n_z)
        return at, {"prow": prow, "pcol": at * 4 + place}

    def q_peer(step):
        at = lax.rem(q + step, 8)
        return at, {"prow": (at // 4) * n_y + y, "pcol": z * 4 + lax.rem(at, 4)}

    def y_peer(step):
        at = lax.rem(y + step, n_y)
        return at, {"prow": x_lo * n_y + at, "pcol": pcol}

    groups = ((z_peer, n_z), (q_peer, 8), (y_peer, n_y))
    barrier = pltpu.get_barrier_semaphore()
    for peer, count in groups:
        for step in range(1, count):
            pl.semaphore_signal(barrier, inc=1, device_id=peer(step)[1], device_id_type=MESH)

    piv_copy.wait()
    pivot = piv_buf[...]
    block = pivot // rows_dev
    offset = (pivot - block * rows_dev).astype(f32)
    own = jnp.where(block == prow * n_pcol + pcol, offset, 0.0)
    own_offset = jnp.sum(jnp.sum(own, axis=0, keepdims=True), axis=1, keepdims=True)
    lane = lax.broadcasted_iota(i32, (16, rows_dev), 1).astype(f32)
    pick = jnp.where(lane == own_offset, 1.0, 0.0).astype(bf16)
    own_copy.wait()
    own_row = jnp.dot(pick, p_out[z, place], preferred_element_type=f32)
    z_rows[z] = own_row[0:1, :]
    at_prow, at_pcol = block // n_pcol, lax.rem(block, n_pcol)
    at_q = (at_prow // n_y) * 4 + lax.rem(at_pcol, 4)
    a_at = (lax.rem(at_prow, n_y) * 8 + at_q) * n_z + at_pcol // 4
    for half in range(2):
        for target, where_from in ((work, block), (order, a_at)):
            value = where_from[half:half + 1, :].astype(f32)
            turned = jnp.transpose(jnp.broadcast_to(value, (128, 128)))
            for part in range(2):
                lane = lax.broadcasted_iota(i32, (128, 128), 1).astype(f32) + 128 * part
                first = 256 + 128 * part if target is work else 128 * part
                target[128 * half:128 * half + 128, first:first + 128] = jnp.where(
                    turned == lane, 1.0, 0.0
                ).astype(target.dtype)
    sub = lax.broadcasted_iota(i32, (n_pcol, 128), 0) + prow * n_pcol
    found = jnp.where(block[0:1, :] == sub, offset[0:1, :], 0.0) + jnp.where(
        block[1:2, :] == sub, offset[1:2, :], 0.0
    )
    row_at = jnp.sum(found, axis=1, keepdims=True) + (
        lax.broadcasted_iota(i32, (n_pcol, 1), 0) * rows_dev
    ).astype(f32)
    chosen = jnp.zeros((n_pcol, trailing.shape[1]), f32)
    for part in range(T_PARTS):
        t_copy(part).wait()
        lane = lax.broadcasted_iota(i32, (n_pcol, part_rows), 1).astype(f32) + part * part_rows
        pick = jnp.where(lane == row_at, 1.0, 0.0).astype(bf16)
        chosen = chosen + jnp.dot(
            pick, t_buf[part * part_rows:(part + 1) * part_rows, :], preferred_element_type=f32
        )
    c_out[x_lo, y] = chosen.astype(bf16)

    pl.semaphore_wait(barrier, n_z - 1 + 7 + n_y - 1)

    def a_copy(stage, ref, slot, target):
        return pltpu.make_async_remote_copy(
            src_ref=ref.at[slot], dst_ref=ref.at[slot],
            send_sem=a_send.at[stage], recv_sem=a_recv.at[stage],
            device_id=target, device_id_type=MESH,
        )

    def a_start(stage, ref, slot):
        peer, count = groups[stage]
        for step in range(1, count):
            a_copy(stage, ref, slot, peer(step)[1]).start()

    def a_all(stage, ref):
        return a_copy(stage, ref, pl.ds(0, groups[stage][1] - 1), groups[stage][0](1)[1])

    def z_copy(slot, target):
        return pltpu.make_async_remote_copy(
            src_ref=p_out.at[slot, place], dst_ref=p_out.at[slot, place],
            send_sem=z_send.at[target], recv_sem=z_recv.at[slot],
            device_id={"prow": prow, "pcol": target * 4 + place}, device_id_type=MESH,
        )

    def x_copy(slot, at_place):
        return pltpu.make_async_remote_copy(
            src_ref=p_out.at[slot, at_place], dst_ref=p_out.at[slot, at_place],
            send_sem=x_send.at[slot], recv_sem=x_recv.at[slot],
            device_id={"prow": prow, "pcol": z * 4 + (1 - x_hi) * 2 + core},
            device_id_type=MESH,
        )

    def sib_copy(slot, at_place):
        return pltpu.make_async_remote_copy(
            src_ref=p_out.at[:, at_place], dst_ref=p_out.at[:, at_place],
            send_sem=sib_send.at[slot], recv_sem=sib_recv.at[slot],
            device_id={"prow": prow, "pcol": z * 4 + x_hi * 2 + (1 - core)},
            device_id_type=MESH,
        )

    def c_copy(at_x, at_y, number, slot, target):
        return pltpu.make_async_remote_copy(
            src_ref=c_out.at[at_x, at_y], dst_ref=c_out.at[at_x, at_y],
            send_sem=c_send.at[number], recv_sem=c_recv.at[slot],
            device_id=target, device_id_type=MESH,
        )

    x_other = {"prow": (1 - x_lo) * n_y + y, "pcol": pcol}

    def c_x_copy(at_x):
        return c_copy(at_x, y, 0, 0, x_other)

    def c_y_copy(at_x, at_y, number, step):
        return c_copy(
            at_x, at_y, 1 + number * n_y + step, 1 + number * n_y + at_y, y_peer(step)[1]
        )

    a_start(0, z_rows, z)
    a_all(0, z_rows).wait_recv()
    q_rows[q] = z_rows[:, 0, :]
    a_start(1, q_rows, q)
    near = [1, n_z - 1, 2, n_z - 2, 3, n_z - 3, 4][: n_z - 1]
    for step in near:
        z_copy(z, lax.rem(z + step, n_z)).start()
    a_all(1, q_rows).wait_recv()
    y_rows[y] = q_rows[...].reshape(8 * n_z, 256).astype(bf16)
    a_start(2, y_rows, y)
    c_x_copy(x_lo).start()
    x_copy(z, place).start()
    a_all(2, y_rows).wait_recv()
    work[:, :256] = jnp.dot(
        order[...], y_rows[...].reshape(256, 256), preferred_element_type=f32
    )
    for step in range(1, n_y):
        c_y_copy(x_lo, y, 0, step).start()

    def pass_on(step):
        slot = lax.rem(z + n_z - step, n_z)
        z_copy(slot, z).wait_recv()
        x_copy(slot, place).start()

    def pass_chosen():
        c_x_copy(1 - x_lo).wait_recv()
        for step in range(1, n_y):
            c_y_copy(1 - x_lo, y, 1, step).start()

    other = (1 - x_hi) * 2 + core
    hooks = {
        1: [pass_chosen],
        2: [lambda: pass_on(near[0]), lambda: pass_on(near[1])],
        3: [lambda: pass_on(near[2]), lambda: pass_on(near[3])],
        4: [lambda: pass_on(near[4]), lambda: pass_on(near[5])],
        5: [lambda: pass_on(near[6])],
        6: [lambda: sib_copy(0, place).start()],
    }
    eliminate(work, rhs, lower_inv, 16, hooks)
    full_inv[...] = work[:, 256:]

    for slot in range(n_z):
        x_copy(slot, other).wait_recv()
    sib_copy(1, other).start()
    for step in range(1, n_y):
        at = lax.rem(y + n_y - step, n_y)
        c_y_copy(x_lo, at, 0, step).wait_recv()
        c_y_copy(1 - x_lo, at, 1, step).wait_recv()
    sib_copy(0, x_hi * 2 + 1 - core).wait_recv()
    sib_copy(1, (1 - x_hi) * 2 + 1 - core).wait_recv()

    for stage, ref in enumerate((z_rows, q_rows, y_rows)):
        a_all(stage, ref).wait_send()
    for step in near:
        z_copy(z, lax.rem(z + step, n_z)).wait_send()
    for slot in range(n_z):
        x_copy(slot, place).wait_send()
    sib_copy(0, place).wait_send()
    sib_copy(1, other).wait_send()
    c_x_copy(x_lo).wait_send()
    for step in range(1, n_y):
        c_y_copy(x_lo, y, 0, step).wait_send()
        c_y_copy(1 - x_lo, y, 1, step).wait_send()


def factor(n_prow, n_pcol, pivots, panels, trailing):
    rows_dev, width = panels.shape
    n_z, n_y = n_pcol // 4, n_prow // 2
    columns = trailing.shape[1]
    dma = pltpu.SemaphoreType.DMA
    vmem, hbm = pl.BlockSpec(memory_space=pltpu.VMEM), pl.BlockSpec(memory_space=pltpu.HBM)
    pivots, panels, trailing = (
        pltpu.with_memory_space_constraint(x, pltpu.HBM) for x in (pivots, panels, trailing)
    )
    return pl.pallas_call(
        functools.partial(factor_kernel, n_prow, n_pcol),
        out_shape=[
            jax.ShapeDtypeStruct((width, width), f32),
            jax.ShapeDtypeStruct((width, width), f32),
            jax.ShapeDtypeStruct((2, n_y, n_pcol, columns), bf16),
            jax.ShapeDtypeStruct((n_z, 4, rows_dev, width), bf16),
        ],
        in_specs=[hbm] * 3,
        out_specs=[vmem] * 4,
        scratch_shapes=[
            pltpu.VMEM(trailing.shape, bf16),
            pltpu.VMEM(pivots.shape, i32),
            pltpu.VMEM((n_z, 1, width), f32),
            pltpu.VMEM((8, n_z, width), f32),
            pltpu.VMEM((n_y, 8 * n_z, width), bf16),
            pltpu.VMEM((width, 2 * width), f32),
            pltpu.VMEM((width, width), bf16),
            pltpu.VMEM((2, width, 2 * width), bf16),
            dma((T_PARTS,)), dma((2,)),
            dma((3,)), dma((3,)),
            dma((n_z,)), dma((n_z,)), dma((n_z,)), dma((n_z,)),
            dma((2,)), dma((2,)),
            dma((1 + 2 * n_y,)), dma((1 + 2 * n_y,)),
        ],
        compiler_params=pltpu.CompilerParams(
            collective_id=0, has_side_effects=True, vmem_limit_bytes=32 * 1024 * 1024
        ),
        name="factor_rows",
    )(pivots, panels, trailing)


def block_elimination(rows, first, extent):
    sub = lax.broadcasted_iota(i32, (extent, 128), 0)
    piece, lane = divmod(first, 128)

    def across(x, k):
        return jnp.broadcast_to(x[k:k + 1, :], (extent, 128))

    columns = [
        jnp.broadcast_to(rows[piece][:, lane + k:lane + k + 1], (extent, 128))
        for k in range(extent)
    ]
    upper = []
    inverse = jnp.zeros((extent, 128), f32)
    for k in range(extent):
        reciprocal = 1.0 / across(columns[k], k)
        factor = jnp.where(sub == k, 0.0, columns[k] * reciprocal)
        inverse = jnp.where(sub == k, reciprocal, inverse)
        upper.append([x[k:k + 1, :] for x in rows[2:]])
        for later in range(k + 1, extent):
            columns[later] = columns[later] - factor * across(columns[later], k)
        rows = [x - factor * across(x, k) for x in rows]
    return [x * inverse for x in rows], upper


def eliminate(work, rhs, lower_inv, extent, hooks):
    rhs[...] = jnp.zeros_like(rhs)
    for first in range(0, 256, extent):
        piece, lane = divmod(first, 128)
        block = slice(first, first + extent)
        rows = [work[block, 128 * q:128 * q + 128] for q in range(4)]
        for hook in hooks.get(first // extent, []):
            hook()
        rows, upper = block_elimination(rows, first, extent)
        for k in range(extent):
            for q in range(2):
                lower_inv[first + k:first + k + 1, 128 * q:128 * q + 128] = upper[k][q]
        high, low = split(work[:, 128 * piece:128 * piece + 128])
        left = jnp.concatenate([high, low], axis=1)
        live = [q for q in range(4) if (q + 1) * 128 > first]
        at = (slice(lane, lane + extent), slice(128 + lane, 128 + lane + extent))
        for q in live:
            for part, value in enumerate(split(rows[q])):
                for place in at:
                    rhs[part, place, 128 * q:128 * q + 128] = value
        for half in range(2):
            if half == 0 and first + extent >= 256:
                continue
            columns = slice(256 * half, 256 * half + 256)
            work[:, columns] = work[:, columns] - (
                jnp.dot(left, rhs[0, :, columns], preferred_element_type=f32)
                + jnp.dot(left, rhs[1, :, columns], preferred_element_type=f32)
            )
        for q in live:
            work[block, 128 * q:128 * q + 128] = rows[q]
            for part in range(2):
                for place in at:
                    rhs[part, place, 128 * q:128 * q + 128] = jnp.zeros((extent, 128), bf16)


def solve_kernel(
    lower_inv, full_inv, chosen, panels, trailing, updated, upper_rows, x_buf, o_buf, o_sem
):
    part_rows = trailing.shape[0] // OUT_PARTS

    def o_copy(part):
        at = pl.ds(part * part_rows, part_rows)
        return pltpu.make_async_copy(o_buf.at[at], updated.at[at], o_sem.at[part])

    def product(left, right):
        high, low = split(left)
        return jnp.dot(high, right, preferred_element_type=f32) + jnp.dot(
            low, right, preferred_element_type=f32
        )

    x_buf[...] = product(full_inv[...], chosen[...]).astype(bf16)
    for part in range(OUT_PARTS):
        at = slice(part * part_rows, (part + 1) * part_rows)
        o_buf[at, :] = (
            trailing[at, :].astype(f32)
            - jnp.dot(panels[at, :], x_buf[...], preferred_element_type=f32)
        ).astype(bf16)
        o_copy(part).start()
    upper_rows[...] = product(lower_inv[...], chosen[...]).astype(bf16)
    for part in range(OUT_PARTS):
        o_copy(part).wait()


def solve(lower_inv, full_inv, chosen, panels, trailing):
    width, columns = chosen.shape
    vmem = pl.BlockSpec(memory_space=pltpu.VMEM)
    return pl.pallas_call(
        solve_kernel,
        out_shape=[
            jax.ShapeDtypeStruct(trailing.shape, bf16),
            jax.ShapeDtypeStruct((width, columns), bf16),
        ],
        in_specs=[vmem] * 5,
        out_specs=[pl.BlockSpec(memory_space=pl.ANY), vmem],
        scratch_shapes=[
            pltpu.VMEM((width, columns), bf16),
            pltpu.VMEM(trailing.shape, bf16),
            pltpu.SemaphoreType.DMA((OUT_PARTS,)),
        ],
        compiler_params=pltpu.CompilerParams(vmem_limit_bytes=32 * 1024 * 1024),
        name="solve_update",
    )(lower_inv, full_inv, chosen, panels, trailing)


def solution(mesh):
    n_prow, n_pcol = mesh.shape["prow"], mesh.shape["pcol"]

    def local(panels, pivots, trailing):
        lower_inv, full_inv, chosen, rows = factor(n_prow, n_pcol, pivots, panels, trailing)
        width = panels.shape[1]
        updated, upper_rows = solve(
            lower_inv, full_inv, chosen.reshape(width, trailing.shape[1]),
            rows.reshape(trailing.shape[0], width), trailing,
        )
        return updated, upper_rows

    return jax.shard_map(
        local,
        mesh=mesh,
        in_specs=(P(("prow", "pcol"), None), P(), P("prow", "pcol")),
        out_specs=(P("prow", "pcol"), P(None, "pcol")),
        check_vma=False,
    )
```

time: 53.8 us -> 39.6 us (0.74)
  Pallas kernels: 49.3 us -> 38.9 us
  local copies, waits for them, and re-layouts: 3.62 us -> 0.01 us
    pallas_call x2, Pallas kernels: 49.3 us -> 38.9 us  [the longest x1 35.4 us: factor(): pl.pallas_call(functools.partial(factor_kernel, n_prow, n_pcol), out_shap...]
    unnamed x10 -> x2, local copies, waits for them, and re-layouts: 3.62 us -> 0.01 us
where the time goes in v2:
time: 39.6 us
  Pallas kernels  38.9 us (98%)
  between operations  0.65 us (2%)
    pallas_call x1, Pallas kernels, factor(): pl.pallas_call(functools.partial(factor_kernel, n_prow, n_pcol), out_shap...  35.4 us
    pallas_call x1, Pallas kernels, solve(): pl.pallas_call(solve_kernel, out_shape=[jax.ShapeDtypeStruct(trailing.sha...  3.52 us

profile of v2, /device:TPU:1, one launch (start us, length us, event | category | flops | bytes accessed | tf_op | source)
XLA Modules:
  0.0 39.6 jit_solution(4821610299023171094)
XLA Ops:
  0.6 0.0 copy-start
  0.6 35.4 %factor_rows.1 = (f32[256,256]{1,0:T(8,128)S(1)}, f32[256,256]{1,0:T(8,128)S(1)}, bf16[2,4,32,1024]{3,2,1,0:T(8,128)(2,1)S(1)}, bf16[8,4,64,256]{3,2,1,0:T(8,128)(2,1)S(1)}) custom-call(s32[2,128]{1,0:T(2,128)} %pivots.1, bf16[64,256]{1,0:T(8,128)(2,1)} %panels.1, bf16[2048,1024]{1,0:T(8,128)(2,1)} %trailing.3), custom_call_target="tpu_custom_call" | custom-call | tf_op jit(solution)/shard_map/factor_rows/pallas_call | solution.py:237
  36.0 0.0 copy-done
  36.0 3.5 %solve_update.1 = (bf16[2048,1024]{1,0:T(8,128)(2,1)}, bf16[256,1024]{1,0:T(8,128)(2,1)}) custom-call(f32[256,256]{1,0:T(8,128)S(1)} %get-tuple-element.6.lower_inv, f32[256,256]{1,0:T(8,128)S(1)} %get-tuple-element.7.full_inv, bf16[256,1024]{1,0:T(8,128)(2,1)S(1)} %bitcast.3, bf16[2048,256]{1,0:T(8,128)(2,1)S(1)} %bitcast.2, bf16[2048,1024]{1,0:T(8,128)(2,1)S(1)} %copy-done), custom_call_target="tpu_custom_call" | custom-call | tf_op jit(solution)/shard_map/solve_update/pallas_call | solution.py:359
Async XLA Ops:
  0.6 35.4 %copy-start = (bf16[2048,1024]{1,0:T(8,128)(2,1)S(1)}, bf16[2048,1024]{1,0:T(8,128)(2,1)}, u32[]{:S(2)}) copy-start(bf16[2048,1024]{1,0:T(8,128)(2,1)} %trailing.3) | copy-start | bytes 12582916

commit v3 on v2

v3 whole, which is shorter than its diff:
```python
import functools

import jax
import jax.numpy as jnp
from jax import lax
from jax.experimental import pallas as pl
from jax.experimental.pallas import tpu as pltpu
from jax.sharding import PartitionSpec as P

f32, bf16, i32 = jnp.float32, jnp.bfloat16, jnp.int32
MESH = pl.DeviceIdType.MESH
T_PARTS = 4
OUT_PARTS = 8


def split(x):
    high = x.astype(bf16)
    return high, (x - high.astype(f32)).astype(bf16)


def factor_kernel(
    n_prow, n_pcol, pivots, panels, trailing, lower_inv, full_inv, c_out, p_out,
    t_buf, piv_buf, g_rows, h_rows, work, order,
    t_sem, in_sem, a_send, a_recv, z_send, z_recv, x_send, x_recv, sib_send, sib_recv,
    c_send, c_recv,
):
    n_z, n_y = n_pcol // 4, n_prow // 2
    prow, pcol = lax.axis_index("prow"), lax.axis_index("pcol")
    x_lo, y = prow // n_y, lax.rem(prow, n_y)
    z, place = pcol // 4, lax.rem(pcol, 4)
    x_hi, core = place // 2, lax.rem(place, 2)
    g, h = z * 2 + core, (x_lo * 2 + x_hi) * n_y + y
    rows_dev = panels.shape[0]
    part_rows = trailing.shape[0] // T_PARTS

    def t_copy(part):
        at = pl.ds(part * part_rows, part_rows)
        return pltpu.make_async_copy(trailing.at[at], t_buf.at[at], t_sem.at[part])

    piv_copy = pltpu.make_async_copy(pivots, piv_buf, in_sem.at[0])
    own_copy = pltpu.make_async_copy(panels, p_out.at[z, place], in_sem.at[1])
    piv_copy.start()
    own_copy.start()
    for part in range(T_PARTS):
        t_copy(part).start()

    def g_peer(step):
        at = lax.rem(g + step, 2 * n_z)
        return {"prow": prow, "pcol": (at // 2) * 4 + x_hi * 2 + lax.rem(at, 2)}

    def h_peer(step):
        at = lax.rem(h + step, 4 * n_y)
        at_x = at // n_y
        return {
            "prow": (at_x // 2) * n_y + lax.rem(at, n_y),
            "pcol": z * 4 + lax.rem(at_x, 2) * 2 + core,
        }

    def y_peer(step):
        return {"prow": x_lo * n_y + lax.rem(y + step, n_y), "pcol": pcol}

    groups = ((g_peer, 2 * n_z), (h_peer, 4 * n_y))
    barrier = pltpu.get_barrier_semaphore()
    for peer, count in groups:
        for step in range(1, count):
            pl.semaphore_signal(barrier, inc=1, device_id=peer(step), device_id_type=MESH)

    piv_copy.wait()
    pivot = piv_buf[...]
    block = pivot // rows_dev
    offset = (pivot - block * rows_dev).astype(f32)
    own = jnp.where(block == prow * n_pcol + pcol, offset, 0.0)
    own_offset = jnp.sum(jnp.sum(own, axis=0, keepdims=True), axis=1, keepdims=True)
    lane = lax.broadcasted_iota(i32, (16, rows_dev), 1).astype(f32)
    pick = jnp.where(lane == own_offset, 1.0, 0.0).astype(bf16)
    own_copy.wait()
    own_row = jnp.dot(pick, p_out[z, place], preferred_element_type=f32)
    g_rows[g] = own_row[0:1, :]
    pl.semaphore_wait(barrier, 2 * n_z - 1 + 4 * n_y - 1)

    def a_copy(stage, ref, slot, target):
        return pltpu.make_async_remote_copy(
            src_ref=ref.at[slot], dst_ref=ref.at[slot],
            send_sem=a_send.at[stage], recv_sem=a_recv.at[stage],
            device_id=target, device_id_type=MESH,
        )

    def a_start(stage, ref, slot):
        peer, count = groups[stage]
        for step in range(1, count):
            a_copy(stage, ref, slot, peer(step)).start()

    def a_all(stage, ref):
        return a_copy(stage, ref, pl.ds(0, groups[stage][1] - 1), groups[stage][0](1))

    def z_copy(slot, target):
        return pltpu.make_async_remote_copy(
            src_ref=p_out.at[slot, place], dst_ref=p_out.at[slot, place],
            send_sem=z_send.at[target], recv_sem=z_recv.at[slot],
            device_id={"prow": prow, "pcol": target * 4 + place}, device_id_type=MESH,
        )

    def x_copy(slot, at_place):
        return pltpu.make_async_remote_copy(
            src_ref=p_out.at[slot, at_place], dst_ref=p_out.at[slot, at_place],
            send_sem=x_send.at[slot], recv_sem=x_recv.at[slot],
            device_id={"prow": prow, "pcol": z * 4 + (1 - x_hi) * 2 + core},
            device_id_type=MESH,
        )

    def sib_copy(slot, at_place):
        return pltpu.make_async_remote_copy(
            src_ref=p_out.at[:, at_place], dst_ref=p_out.at[:, at_place],
            send_sem=sib_send.at[slot], recv_sem=sib_recv.at[slot],
            device_id={"prow": prow, "pcol": z * 4 + x_hi * 2 + (1 - core)},
            device_id_type=MESH,
        )

    def c_copy(at_x, at_y, number, slot, target):
        return pltpu.make_async_remote_copy(
            src_ref=c_out.at[at_x, at_y], dst_ref=c_out.at[at_x, at_y],
            send_sem=c_send.at[number], recv_sem=c_recv.at[slot],
            device_id=target, device_id_type=MESH,
        )

    x_other = {"prow": (1 - x_lo) * n_y + y, "pcol": pcol}

    def c_x_copy(at_x):
        return c_copy(at_x, y, 0, 0, x_other)

    def c_y_copy(at_x, at_y, number, step):
        return c_copy(
            at_x, at_y, 1 + number * n_y + step, 1 + number * n_y + at_y, y_peer(step)
        )

    def pass_on(step):
        slot = lax.rem(z + n_z - step, n_z)
        z_copy(slot, z).wait_recv()
        x_copy(slot, place).start()

    a_start(0, g_rows, g)
    near = [1, n_z - 1, 2, n_z - 2, 3, n_z - 3, 4][: n_z - 1]
    for step in near:
        z_copy(z, lax.rem(z + step, n_z)).start()
    x_copy(z, place).start()
    at_prow, at_pcol = block // n_pcol, lax.rem(block, n_pcol)
    at_x = (at_prow // n_y) * 2 + lax.rem(at_pcol, 4) // 2
    at_h = at_x * n_y + lax.rem(at_prow, n_y)
    a_at = (at_h * n_z + at_pcol // 4) * 2 + lax.rem(at_pcol, 2)
    for half in range(2):
        for target, where_from in ((work, block), (order, a_at)):
            value = where_from[half:half + 1, :].astype(f32)
            turned = jnp.transpose(jnp.broadcast_to(value, (128, 128)))
            for part in range(2):
                lane = lax.broadcasted_iota(i32, (128, 128), 1).astype(f32) + 128 * part
                first = 256 + 128 * part if target is work else 128 * part
                target[128 * half:128 * half + 128, first:first + 128] = jnp.where(
                    turned == lane, 1.0, 0.0
                ).astype(target.dtype)
    a_all(0, g_rows).wait_recv()
    h_rows[h] = g_rows[:, 0, :].astype(bf16)
    a_start(1, h_rows, h)
    sub = lax.broadcasted_iota(i32, (n_pcol, 128), 0) + prow * n_pcol
    found = jnp.where(block[0:1, :] == sub, offset[0:1, :], 0.0) + jnp.where(
        block[1:2, :] == sub, offset[1:2, :], 0.0
    )
    row_at = jnp.sum(found, axis=1, keepdims=True) + (
        lax.broadcasted_iota(i32, (n_pcol, 1), 0) * rows_dev
    ).astype(f32)
    chosen = jnp.zeros((n_pcol, trailing.shape[1]), f32)
    for part in range(T_PARTS):
        t_copy(part).wait()
        lane = lax.broadcasted_iota(i32, (n_pcol, part_rows), 1).astype(f32) + part * part_rows
        pick = jnp.where(lane == row_at, 1.0, 0.0).astype(bf16)
        chosen = chosen + jnp.dot(
            pick, t_buf[part * part_rows:(part + 1) * part_rows, :], preferred_element_type=f32
        )
    c_out[x_lo, y] = chosen.astype(bf16)
    c_x_copy(x_lo).start()
    pass_on(near[0])
    pass_on(near[1])
    a_all(1, h_rows).wait_recv()
    for step in range(1, n_y):
        c_y_copy(x_lo, y, 0, step).start()
    for step in near[2:]:
        pass_on(step)
    sib_copy(0, place).start()
    work[:, :256] = jnp.dot(
        order[...], h_rows[...].reshape(256, 256), preferred_element_type=f32
    )

    def pass_chosen():
        c_x_copy(1 - x_lo).wait_recv()
        for step in range(1, n_y):
            c_y_copy(1 - x_lo, y, 1, step).start()

    other = (1 - x_hi) * 2 + core
    def pass_far():
        for slot in range(n_z):
            x_copy(slot, other).wait_recv()
        sib_copy(1, other).start()

    hooks = {5: [pass_chosen], 9: [pass_far]}
    eliminate(work, lower_inv, 16, hooks)
    full_inv[...] = work[:, 256:]

    for step in range(1, n_y):
        at = lax.rem(y + n_y - step, n_y)
        c_y_copy(x_lo, at, 0, step).wait_recv()
        c_y_copy(1 - x_lo, at, 1, step).wait_recv()
    sib_copy(0, x_hi * 2 + 1 - core).wait_recv()
    sib_copy(1, (1 - x_hi) * 2 + 1 - core).wait_recv()

    for stage, ref in enumerate((g_rows, h_rows)):
        a_all(stage, ref).wait_send()
    for step in near:
        z_copy(z, lax.rem(z + step, n_z)).wait_send()
    for slot in range(n_z):
        x_copy(slot, place).wait_send()
    sib_copy(0, place).wait_send()
    sib_copy(1, other).wait_send()
    c_x_copy(x_lo).wait_send()
    for step in range(1, n_y):
        c_y_copy(x_lo, y, 0, step).wait_send()
        c_y_copy(1 - x_lo, y, 1, step).wait_send()


def factor(n_prow, n_pcol, pivots, panels, trailing):
    rows_dev, width = panels.shape
    n_z, n_y = n_pcol // 4, n_prow // 2
    columns = trailing.shape[1]
    dma = pltpu.SemaphoreType.DMA
    vmem, hbm = pl.BlockSpec(memory_space=pltpu.VMEM), pl.BlockSpec(memory_space=pltpu.HBM)
    pivots, panels, trailing = (
        pltpu.with_memory_space_constraint(x, pltpu.HBM) for x in (pivots, panels, trailing)
    )
    return pl.pallas_call(
        functools.partial(factor_kernel, n_prow, n_pcol),
        out_shape=[
            jax.ShapeDtypeStruct((width, width), f32),
            jax.ShapeDtypeStruct((width, width), f32),
            jax.ShapeDtypeStruct((2, n_y, n_pcol, columns), bf16),
            jax.ShapeDtypeStruct((n_z, 4, rows_dev, width), bf16),
        ],
        in_specs=[hbm] * 3,
        out_specs=[vmem] * 4,
        scratch_shapes=[
            pltpu.VMEM(trailing.shape, bf16),
            pltpu.VMEM(pivots.shape, i32),
            pltpu.VMEM((2 * n_z, 1, width), f32),
            pltpu.VMEM((4 * n_y, 2 * n_z, width), bf16),
            pltpu.VMEM((width, 2 * width), f32),
            pltpu.VMEM((width, width), bf16),
            dma((T_PARTS,)), dma((2,)),
            dma((2,)), dma((2,)),
            dma((n_z,)), dma((n_z,)), dma((n_z,)), dma((n_z,)),
            dma((2,)), dma((2,)),
            dma((1 + 2 * n_y,)), dma((1 + 2 * n_y,)),
        ],
        compiler_params=pltpu.CompilerParams(
            collective_id=0, has_side_effects=True, vmem_limit_bytes=32 * 1024 * 1024
        ),
        name="factor_rows",
    )(pivots, panels, trailing)


def eliminate(work, lower_inv, extent, hooks):
    total = 256
    shape = (extent, 128)
    sub = lax.broadcasted_iota(i32, shape, 0)
    lanes = lax.broadcasted_iota(i32, (total, 128), 1)

    def across(x, k):
        return jnp.broadcast_to(x[k:k + 1, :], shape)

    def column(rows, at):
        piece, lane = divmod(at, 128)
        return jnp.broadcast_to(rows[piece][:, lane:lane + 1], shape)

    def load(first):
        return [work[first:first + extent, 128 * q:128 * q + 128] for q in range(4)]

    rows = load(0)
    for first in range(0, total, extent):
        for hook in hooks.get(first // extent, []):
            hook()
        piece, lane = divmod(first, 128)
        after = first + extent
        last = after >= total
        live = [q for q in range(4) if (q + 1) * 128 > after]
        columns = [column(rows, first + k) for k in range(extent)]
        if not last:
            ahead = load(after)
            ahead_columns = [column(ahead, first + k) for k in range(extent)]
        inverse = jnp.zeros(shape, f32)
        upper = [jnp.zeros(shape, f32)] * 2
        for k in range(extent):
            reciprocal = 1.0 / across(columns[k], k)
            factor = jnp.where(sub == k, 0.0, columns[k] * reciprocal)
            inverse = jnp.where(sub == k, reciprocal, inverse)
            upper = [jnp.where(sub == k, rows[2 + q], upper[q]) for q in range(2)]
            pivot_row = {q: across(rows[q], k) for q in live}
            pivot_columns = [across(columns[j], k) for j in range(k + 1, extent)]
            if not last:
                times = ahead_columns[k] * reciprocal
                for j in range(k + 1, extent):
                    ahead_columns[j] = ahead_columns[j] - times * pivot_columns[j - k - 1]
                for q in live:
                    ahead[q] = ahead[q] - times * pivot_row[q]
            for j in range(k + 1, extent):
                columns[j] = columns[j] - factor * pivot_columns[j - k - 1]
            for q in live:
                rows[q] = rows[q] - factor * pivot_row[q]
        rows = [x * inverse for x in rows]
        for q in range(2):
            lower_inv[first:after, 128 * q:128 * q + 128] = upper[q]
        group = work[:, 128 * piece:128 * piece + 128]
        high = group.astype(bf16).astype(f32)
        low = group - high
        second, third = (lane + extent) % 128, (lane + 2 * extent) % 128
        left = jnp.where(
            (lanes >= lane) & (lanes < lane + extent), high,
            jnp.where((lanes >= second) & (lanes < second + extent), pltpu.roll(low, extent, 1),
                      pltpu.roll(high, 2 * extent, 1)),
        ).astype(bf16)
        blank = jnp.zeros(shape, bf16)
        for pair in [live[:-2], live[-2:]] if len(live) > 2 else [live]:
            tiles = []
            for p in pair:
                xh, xl = split(rows[p])
                parts = [blank] * (128 // extent)
                parts[lane // extent], parts[second // extent], parts[third // extent] = xh, xh, xl
                tiles.append(jnp.concatenate(parts, axis=0))
            right = jnp.concatenate(tiles, axis=1) if len(tiles) > 1 else tiles[0]
            cs = slice(128 * pair[0], 128 * (pair[-1] + 1))
            for lo_row, hi_row in ((0, first), (after + extent, total)):
                if hi_row <= lo_row:
                    continue
                work[lo_row:hi_row, cs] = work[lo_row:hi_row, cs] - jnp.dot(
                    left[lo_row:hi_row], right, preferred_element_type=f32)
        for q in live:
            work[first:after, 128 * q:128 * q + 128] = rows[q]
        if not last:
            rows = ahead

def solve_kernel(
    lower_inv, full_inv, chosen, panels, trailing, updated, upper_rows, x_buf, o_buf, o_sem
):
    part_rows = trailing.shape[0] // OUT_PARTS

    def o_copy(part):
        at = pl.ds(part * part_rows, part_rows)
        return pltpu.make_async_copy(o_buf.at[at], updated.at[at], o_sem.at[part])

    def product(left, right):
        high, low = split(left)
        return jnp.dot(high, right, preferred_element_type=f32) + jnp.dot(
            low, right, preferred_element_type=f32
        )

    x_buf[...] = product(full_inv[...], chosen[...]).astype(bf16)
    for part in range(OUT_PARTS):
        at = slice(part * part_rows, (part + 1) * part_rows)
        o_buf[at, :] = (
            trailing[at, :].astype(f32)
            - jnp.dot(panels[at, :], x_buf[...], preferred_element_type=f32)
        ).astype(bf16)
        o_copy(part).start()
    upper_rows[...] = product(lower_inv[...], chosen[...]).astype(bf16)
    for part in range(OUT_PARTS):
        o_copy(part).wait()


def solve(lower_inv, full_inv, chosen, panels, trailing):
    width, columns = chosen.shape
    vmem = pl.BlockSpec(memory_space=pltpu.VMEM)
    return pl.pallas_call(
        solve_kernel,
        out_shape=[
            jax.ShapeDtypeStruct(trailing.shape, bf16),
            jax.ShapeDtypeStruct((width, columns), bf16),
        ],
        in_specs=[vmem] * 5,
        out_specs=[pl.BlockSpec(memory_space=pl.ANY), vmem],
        scratch_shapes=[
            pltpu.VMEM((width, columns), bf16),
            pltpu.VMEM(trailing.shape, bf16),
            pltpu.SemaphoreType.DMA((OUT_PARTS,)),
        ],
        compiler_params=pltpu.CompilerParams(vmem_limit_bytes=32 * 1024 * 1024),
        name="solve_update",
    )(lower_inv, full_inv, chosen, panels, trailing)


def solution(mesh):
    n_prow, n_pcol = mesh.shape["prow"], mesh.shape["pcol"]

    def local(panels, pivots, trailing):
        lower_inv, full_inv, chosen, rows = factor(n_prow, n_pcol, pivots, panels, trailing)
        width = panels.shape[1]
        updated, upper_rows = solve(
            lower_inv, full_inv, chosen.reshape(width, trailing.shape[1]),
            rows.reshape(trailing.shape[0], width), trailing,
        )
        return updated, upper_rows

    return jax.shard_map(
        local,
        mesh=mesh,
        in_specs=(P(("prow", "pcol"), None), P(), P("prow", "pcol")),
        out_specs=(P("prow", "pcol"), P(None, "pcol")),
        check_vma=False,
    )
```

time: 39.6 us -> 33 us (0.83)
  Pallas kernels: 38.9 us -> 32.2 us
    pallas_call x1, Pallas kernels: 35.4 us -> 28.7 us  [factor(): pl.pallas_call(functools.partial(factor_kernel, n_prow, n_pcol), out_shap...]
where the time goes in v3:
time: 33 us; the launch traced here: 32.9 us
  Pallas kernels  32.2 us (98%)
  between operations  0.65 us (2%)
    pallas_call x1, Pallas kernels, factor(): pl.pallas_call(functools.partial(factor_kernel, n_prow, n_pcol), out_shap...  28.7 us
    pallas_call x1, Pallas kernels, solve(): pl.pallas_call(solve_kernel, out_shape=[jax.ShapeDtypeStruct(trailing.sha...  3.52 us

profile of v3, /device:TPU:1, one launch (start us, length us, event | category | flops | bytes accessed | tf_op | source)
XLA Modules:
  0.0 32.9 jit_solution(8873663267669433598)
XLA Ops:
  0.6 0.0 copy-start
  0.6 28.7 %factor_rows.1 = (f32[256,256]{1,0:T(8,128)S(1)}, f32[256,256]{1,0:T(8,128)S(1)}, bf16[2,4,32,1024]{3,2,1,0:T(8,128)(2,1)S(1)}, bf16[8,4,64,256]{3,2,1,0:T(8,128)(2,1)S(1)}) custom-call(s32[2,128]{1,0:T(2,128)} %pivots.1, bf16[64,256]{1,0:T(8,128)(2,1)} %panels.1, bf16[2048,1024]{1,0:T(8,128)(2,1)} %trailing.3), custom_call_target="tpu_custom_call" | custom-call | tf_op jit(solution)/shard_map/factor_rows/pallas_call | solution.py:237
  29.4 0.0 copy-done
  29.4 3.5 %solve_update.1 = (bf16[2048,1024]{1,0:T(8,128)(2,1)}, bf16[256,1024]{1,0:T(8,128)(2,1)}) custom-call(f32[256,256]{1,0:T(8,128)S(1)} %get-tuple-element.6.lower_inv, f32[256,256]{1,0:T(8,128)S(1)} %get-tuple-element.7.full_inv, bf16[256,1024]{1,0:T(8,128)(2,1)S(1)} %bitcast.3, bf16[2048,256]{1,0:T(8,128)(2,1)S(1)} %bitcast.2, bf16[2048,1024]{1,0:T(8,128)(2,1)S(1)} %copy-done), custom_call_target="tpu_custom_call" | custom-call | tf_op jit(solution)/shard_map/solve_update/pallas_call | solution.py:377
Async XLA Ops:
  0.6 28.7 %copy-start = (bf16[2048,1024]{1,0:T(8,128)(2,1)S(1)}, bf16[2048,1024]{1,0:T(8,128)(2,1)}, u32[]{:S(2)}) copy-start(bf16[2048,1024]{1,0:T(8,128)(2,1)} %trailing.3) | copy-start | bytes 12582916

commit v4 on v3

--- a/solution.py
+++ b/solution.py
@@ -21,7 +21,7 @@
 def factor_kernel(
     n_prow, n_pcol, pivots, panels, trailing, lower_inv, full_inv, c_out, p_out,
     t_buf, piv_buf, g_rows, h_rows, work, order,
-    t_sem, in_sem, a_send, a_recv, z_send, z_recv, x_send, x_recv, sib_send, sib_recv,
+    t_sem, in_sem, a_send, a_recv, z_send, z_recv, x_send, x_recv, w_send, w_recv, sib_send, sib_recv,
     c_send, c_recv,
 ):
     n_z, n_y = n_pcol // 4, n_prow // 2
@@ -30,6 +30,7 @@
     z, place = pcol // 4, lax.rem(pcol, 4)
     x_hi, core = place // 2, lax.rem(place, 2)
     g, h = z * 2 + core, (x_lo * 2 + x_hi) * n_y + y
+    other = (1 - x_hi) * 2 + core
     rows_dev = panels.shape[0]
     part_rows = trailing.shape[0] // T_PARTS
 
@@ -45,24 +46,37 @@
         t_copy(part).start()
 
     def g_peer(step):
-        at = lax.rem(g + step, 2 * n_z)
-        return {"prow": prow, "pcol": (at // 2) * 4 + x_hi * 2 + lax.rem(at, 2)}
+        to_z, to_core = step
+        at_z, at_core = lax.rem(z + to_z, n_z), lax.rem(core + to_core, 2)
+        return {"prow": prow, "pcol": at_z * 4 + x_hi * 2 + at_core}
 
     def h_peer(step):
-        at = lax.rem(h + step, 4 * n_y)
-        at_x = at // n_y
+        to_hi, to_lo, to_y = step
+        at_hi, at_lo = lax.rem(x_hi + to_hi, 2), lax.rem(x_lo + to_lo, 2)
         return {
-            "prow": (at_x // 2) * n_y + lax.rem(at, n_y),
-            "pcol": z * 4 + lax.rem(at_x, 2) * 2 + core,
+            "prow": at_lo * n_y + lax.rem(y + to_y, n_y),
+            "pcol": z * 4 + at_hi * 2 + core,
         }
 
     def y_peer(step):
         return {"prow": x_lo * n_y + lax.rem(y + step, n_y), "pcol": pcol}
 
-    groups = ((g_peer, 2 * n_z), (h_peer, 4 * n_y))
+    def hops(distance, around):
+        return min(distance, around - distance)
+
+    g_steps = sorted(
+        ((to_z, to_core) for to_z in range(n_z) for to_core in range(2) if to_z + to_core),
+        key=lambda step: (-hops(step[0], n_z), step),
+    )
+    h_steps = sorted(
+        ((hi, lo, to_y) for hi in range(2) for lo in range(2) for to_y in range(n_y)
+         if hi + lo + to_y),
+        key=lambda step: (-hops(step[2], n_y) - (0, 1, 2, 1)[2 * step[0] + step[1]], step),
+    )
+    groups = ((g_peer, g_steps), (h_peer, h_steps))
     barrier = pltpu.get_barrier_semaphore()
-    for peer, count in groups:
-        for step in range(1, count):
+    for peer, steps in groups:
+        for step in steps:
             pl.semaphore_signal(barrier, inc=1, device_id=peer(step), device_id_type=MESH)
 
     piv_copy.wait()
@@ -86,12 +100,12 @@
         )
 
     def a_start(stage, ref, slot):
-        peer, count = groups[stage]
-        for step in range(1, count):
+        peer, steps = groups[stage]
+        for step in steps:
             a_copy(stage, ref, slot, peer(step)).start()
 
     def a_all(stage, ref):
-        return a_copy(stage, ref, pl.ds(0, groups[stage][1] - 1), groups[stage][0](1))
+        return a_copy(stage, ref, pl.ds(0, len(groups[stage][1])), y_peer(1))
 
     def z_copy(slot, target):
         return pltpu.make_async_remote_copy(
@@ -108,6 +122,13 @@
             device_id_type=MESH,
         )
 
+    def w_copy(slot, target):
+        return pltpu.make_async_remote_copy(
+            src_ref=p_out.at[slot, other], dst_ref=p_out.at[slot, other],
+            send_sem=w_send.at[target], recv_sem=w_recv.at[slot],
+            device_id={"prow": prow, "pcol": target * 4 + place}, device_id_type=MESH,
+        )
+
     def sib_copy(slot, at_place):
         return pltpu.make_async_remote_copy(
             src_ref=p_out.at[:, at_place], dst_ref=p_out.at[:, at_place],
@@ -133,15 +154,13 @@
             at_x, at_y, 1 + number * n_y + step, 1 + number * n_y + at_y, y_peer(step)
         )
 
-    def pass_on(step):
-        slot = lax.rem(z + n_z - step, n_z)
-        z_copy(slot, z).wait_recv()
-        x_copy(slot, place).start()
+    def beside(step):
+        return lax.rem(z + step + n_z, n_z)
 
     a_start(0, g_rows, g)
-    near = [1, n_z - 1, 2, n_z - 2, 3, n_z - 3, 4][: n_z - 1]
-    for step in near:
-        z_copy(z, lax.rem(z + step, n_z)).start()
+    near, far = (1, -1, 2, -2), (3, -3, 4)
+    for step in far + near:
+        z_copy(z, beside(step)).start()
     x_copy(z, place).start()
     at_prow, at_pcol = block // n_pcol, lax.rem(block, n_pcol)
     at_x = (at_prow // n_y) * 2 + lax.rem(at_pcol, 4) // 2
@@ -157,6 +176,9 @@
                 target[128 * half:128 * half + 128, first:first + 128] = jnp.where(
                     turned == lane, 1.0, 0.0
                 ).astype(target.dtype)
+    x_copy(z, other).wait_recv()
+    for step in near:
+        w_copy(z, beside(step)).start()
     a_all(0, g_rows).wait_recv()
     h_rows[h] = g_rows[:, 0, :].astype(bf16)
     a_start(1, h_rows, h)
@@ -177,14 +199,15 @@
         )
     c_out[x_lo, y] = chosen.astype(bf16)
     c_x_copy(x_lo).start()
-    pass_on(near[0])
-    pass_on(near[1])
-    a_all(1, h_rows).wait_recv()
+    for step in far:
+        z_copy(beside(-step), z).wait_recv()
+        x_copy(beside(-step), place).start()
+    for step in near:
+        z_copy(beside(-step), z).wait_recv()
+    sib_copy(0, place).start()
     for step in range(1, n_y):
         c_y_copy(x_lo, y, 0, step).start()
-    for step in near[2:]:
-        pass_on(step)
-    sib_copy(0, place).start()
+    a_all(1, h_rows).wait_recv()
     work[:, :256] = jnp.dot(
         order[...], h_rows[...].reshape(256, 256), preferred_element_type=f32
     )
@@ -194,13 +217,14 @@
         for step in range(1, n_y):
             c_y_copy(1 - x_lo, y, 1, step).start()
 
-    other = (1 - x_hi) * 2 + core
     def pass_far():
-        for slot in range(n_z):
-            x_copy(slot, other).wait_recv()
+        for step in near:
+            w_copy(beside(-step), z).wait_recv()
+        for step in far:
+            x_copy(beside(-step), other).wait_recv()
         sib_copy(1, other).start()
 
-    hooks = {5: [pass_chosen], 9: [pass_far]}
+    hooks = {4: [pass_chosen], 8: [pass_far]}
     eliminate(work, lower_inv, 16, hooks)
     full_inv[...] = work[:, 256:]
 
@@ -213,10 +237,12 @@
 
     for stage, ref in enumerate((g_rows, h_rows)):
         a_all(stage, ref).wait_send()
+    for step in far + near:
+        z_copy(z, beside(step)).wait_send()
     for step in near:
-        z_copy(z, lax.rem(z + step, n_z)).wait_send()
-    for slot in range(n_z):
-        x_copy(slot, place).wait_send()
+        w_copy(z, beside(step)).wait_send()
+    for step in (0,) + far:
+        x_copy(beside(-step), place).wait_send()
     sib_copy(0, place).wait_send()
     sib_copy(1, other).wait_send()
     c_x_copy(x_lo).wait_send()
@@ -253,7 +279,7 @@
             pltpu.VMEM((width, width), bf16),
             dma((T_PARTS,)), dma((2,)),
             dma((2,)), dma((2,)),
-            dma((n_z,)), dma((n_z,)), dma((n_z,)), dma((n_z,)),
+            dma((n_z,)), dma((n_z,)), dma((n_z,)), dma((n_z,)), dma((n_z,)), dma((n_z,)),
             dma((2,)), dma((2,)),
             dma((1 + 2 * n_y,)), dma((1 + 2 * n_y,)),
         ],

time: 33 us -> 31.4 us (0.952)
  Pallas kernels: 32.2 us -> 30.7 us
    pallas_call x1, Pallas kernels: 28.7 us -> 27.2 us  [factor(): pl.pallas_call(functools.partial(factor_kernel, n_prow, n_pcol), out_shap...]
where the time goes in v4:
time: 31.4 us
  Pallas kernels  30.7 us (98%)
  between operations  0.65 us (2%)
    pallas_call x1, Pallas kernels, factor(): pl.pallas_call(functools.partial(factor_kernel, n_prow, n_pcol), out_shap...  27.2 us
    pallas_call x1, Pallas kernels, solve(): pl.pallas_call(solve_kernel, out_shape=[jax.ShapeDtypeStruct(trailing.sha...  3.52 us

profile of v4, /device:TPU:1, one launch (start us, length us, event | category | flops | bytes accessed | tf_op | source)
XLA Modules:
  0.0 31.4 jit_solution(13511875179067320116)
XLA Ops:
  0.6 0.0 copy-start
  0.6 27.2 %factor_rows.1 = (f32[256,256]{1,0:T(8,128)S(1)}, f32[256,256]{1,0:T(8,128)S(1)}, bf16[2,4,32,1024]{3,2,1,0:T(8,128)(2,1)S(1)}, bf16[8,4,64,256]{3,2,1,0:T(8,128)(2,1)S(1)}) custom-call(s32[2,128]{1,0:T(2,128)} %pivots.1, bf16[64,256]{1,0:T(8,128)(2,1)} %panels.1, bf16[2048,1024]{1,0:T(8,128)(2,1)} %trailing.3), custom_call_target="tpu_custom_call" | custom-call | tf_op jit(solution)/shard_map/factor_rows/pallas_call | solution.py:263
  27.8 0.0 copy-done
  27.8 3.5 %solve_update.1 = (bf16[2048,1024]{1,0:T(8,128)(2,1)}, bf16[256,1024]{1,0:T(8,128)(2,1)}) custom-call(f32[256,256]{1,0:T(8,128)S(1)} %get-tuple-element.6.lower_inv, f32[256,256]{1,0:T(8,128)S(1)} %get-tuple-element.7.full_inv, bf16[256,1024]{1,0:T(8,128)(2,1)S(1)} %bitcast.3, bf16[2048,256]{1,0:T(8,128)(2,1)S(1)} %bitcast.2, bf16[2048,1024]{1,0:T(8,128)(2,1)S(1)} %copy-done), custom_call_target="tpu_custom_call" | custom-call | tf_op jit(solution)/shard_map/solve_update/pallas_call | solution.py:403
Async XLA Ops:
  0.6 27.2 %copy-start = (bf16[2048,1024]{1,0:T(8,128)(2,1)S(1)}, bf16[2048,1024]{1,0:T(8,128)(2,1)}, u32[]{:S(2)}) copy-start(bf16[2048,1024]{1,0:T(8,128)(2,1)} %trailing.3) | copy-start | bytes 12582916

commit v5 on v4

--- a/solution.py
+++ b/solution.py
@@ -370,7 +370,7 @@
             rows = ahead
 
 def solve_kernel(
-    lower_inv, full_inv, chosen, panels, trailing, updated, upper_rows, x_buf, o_buf, o_sem
+    lower_inv, full_inv, chosen, panels, trailing, updated, upper_rows, x_buf, u_buf, o_buf, o_sem, u_sem
 ):
     part_rows = trailing.shape[0] // OUT_PARTS
 
@@ -384,6 +384,7 @@
             low, right, preferred_element_type=f32
         )
 
+    u_copy = pltpu.make_async_copy(u_buf, upper_rows, u_sem)
     x_buf[...] = product(full_inv[...], chosen[...]).astype(bf16)
     for part in range(OUT_PARTS):
         at = slice(part * part_rows, (part + 1) * part_rows)
@@ -392,9 +393,12 @@
             - jnp.dot(panels[at, :], x_buf[...], preferred_element_type=f32)
         ).astype(bf16)
         o_copy(part).start()
-    upper_rows[...] = product(lower_inv[...], chosen[...]).astype(bf16)
+        if part == OUT_PARTS // 2:
+            u_buf[...] = product(lower_inv[...], chosen[...]).astype(bf16)
+            u_copy.start()
     for part in range(OUT_PARTS):
         o_copy(part).wait()
+    u_copy.wait()
 
 
 def solve(lower_inv, full_inv, chosen, panels, trailing):
@@ -407,11 +411,13 @@
             jax.ShapeDtypeStruct((width, columns), bf16),
         ],
         in_specs=[vmem] * 5,
-        out_specs=[pl.BlockSpec(memory_space=pl.ANY), vmem],
+        out_specs=[pl.BlockSpec(memory_space=pl.ANY)] * 2,
         scratch_shapes=[
+            pltpu.VMEM((width, columns), bf16),
             pltpu.VMEM((width, columns), bf16),
             pltpu.VMEM(trailing.shape, bf16),
             pltpu.SemaphoreType.DMA((OUT_PARTS,)),
+            pltpu.SemaphoreType.DMA,
         ],
         compiler_params=pltpu.CompilerParams(vmem_limit_bytes=32 * 1024 * 1024),
         name="solve_update",

time: 31.4 us -> 30.8 us (0.981)
  Pallas kernels: 30.7 us -> 30.1 us
    pallas_call x1, Pallas kernels: 3.52 us -> 2.91 us  [solve(): pl.pallas_call(solve_kernel, out_shape=[jax.ShapeDtypeStruct(trailing.sha...]
where the time goes in v5:
time: 30.8 us; the launch traced here: 30.7 us
  Pallas kernels  30.1 us (98%)
  between operations  0.65 us (2%)
    pallas_call x1, Pallas kernels, factor(): pl.pallas_call(functools.partial(factor_kernel, n_prow, n_pcol), out_shap...  27.2 us
    pallas_call x1, Pallas kernels, solve(): pl.pallas_call(solve_kernel, out_shape=[jax.ShapeDtypeStruct(trailing.sha...  2.91 us

profile of v5, /device:TPU:1, one launch (start us, length us, event | category | flops | bytes accessed | tf_op | source)
XLA Modules:
  0.0 30.7 jit_solution(13072947452391314992)
XLA Ops:
  0.6 0.0 copy-start
  0.6 27.2 %factor_rows.1 = (f32[256,256]{1,0:T(8,128)S(1)}, f32[256,256]{1,0:T(8,128)S(1)}, bf16[2,4,32,1024]{3,2,1,0:T(8,128)(2,1)S(1)}, bf16[8,4,64,256]{3,2,1,0:T(8,128)(2,1)S(1)}) custom-call(s32[2,128]{1,0:T(2,128)} %pivots.1, bf16[64,256]{1,0:T(8,128)(2,1)} %panels.1, bf16[2048,1024]{1,0:T(8,128)(2,1)} %trailing.3), custom_call_target="tpu_custom_call" | custom-call | tf_op jit(solution)/shard_map/factor_rows/pallas_call | solution.py:263
  27.8 0.0 copy-done
  27.8 2.9 %solve_update.1 = (bf16[2048,1024]{1,0:T(8,128)(2,1)}, bf16[256,1024]{1,0:T(8,128)(2,1)}) custom-call(f32[256,256]{1,0:T(8,128)S(1)} %get-tuple-element.6.lower_inv, f32[256,256]{1,0:T(8,128)S(1)} %get-tuple-element.7.full_inv, bf16[256,1024]{1,0:T(8,128)(2,1)S(1)} %bitcast.3, bf16[2048,256]{1,0:T(8,128)(2,1)S(1)} %bitcast.2, bf16[2048,1024]{1,0:T(8,128)(2,1)S(1)} %copy-done), custom_call_target="tpu_custom_call" | custom-call | tf_op jit(solution)/shard_map/solve_update/pallas_call | solution.py:407
Async XLA Ops:
  0.6 27.2 %copy-start = (bf16[2048,1024]{1,0:T(8,128)(2,1)S(1)}, bf16[2048,1024]{1,0:T(8,128)(2,1)}, u32[]{:S(2)}) copy-start(bf16[2048,1024]{1,0:T(8,128)(2,1)} %trailing.3) | copy-start | bytes 12582916

commit v6 on v5

--- a/solution.py
+++ b/solution.py
@@ -159,9 +159,9 @@
 
     a_start(0, g_rows, g)
     near, far = (1, -1, 2, -2), (3, -3, 4)
+    x_copy(z, place).start()
     for step in far + near:
         z_copy(z, beside(step)).start()
-    x_copy(z, place).start()
     at_prow, at_pcol = block // n_pcol, lax.rem(block, n_pcol)
     at_x = (at_prow // n_y) * 2 + lax.rem(at_pcol, 4) // 2
     at_h = at_x * n_y + lax.rem(at_prow, n_y)

time: 30.8 us -> 30.8 us (level)
  no operation moved by 1% of the time
where the time goes in v6:
time: 30.8 us; the launch traced here: 30.7 us
  Pallas kernels  30.1 us (98%)
  between operations  0.65 us (2%)
    pallas_call x1, Pallas kernels, factor(): pl.pallas_call(functools.partial(factor_kernel, n_prow, n_pcol), out_shap...  27.2 us
    pallas_call x1, Pallas kernels, solve(): pl.pallas_call(solve_kernel, out_shape=[jax.ShapeDtypeStruct(trailing.sha...  2.91 us

profile of v6, /device:TPU:1, one launch (start us, length us, event | category | flops | bytes accessed | tf_op | source)
XLA Modules:
  0.0 30.7 jit_solution(6631629272120808214)
XLA Ops:
  0.6 0.0 copy-start
  0.6 27.2 %factor_rows.1 = (f32[256,256]{1,0:T(8,128)S(1)}, f32[256,256]{1,0:T(8,128)S(1)}, bf16[2,4,32,1024]{3,2,1,0:T(8,128)(2,1)S(1)}, bf16[8,4,64,256]{3,2,1,0:T(8,128)(2,1)S(1)}) custom-call(s32[2,128]{1,0:T(2,128)} %pivots.1, bf16[64,256]{1,0:T(8,128)(2,1)} %panels.1, bf16[2048,1024]{1,0:T(8,128)(2,1)} %trailing.3), custom_call_target="tpu_custom_call" | custom-call | tf_op jit(solution)/shard_map/factor_rows/pallas_call | solution.py:263
  27.8 0.0 copy-done
  27.8 2.9 %solve_update.1 = (bf16[2048,1024]{1,0:T(8,128)(2,1)}, bf16[256,1024]{1,0:T(8,128)(2,1)}) custom-call(f32[256,256]{1,0:T(8,128)S(1)} %get-tuple-element.6.lower_inv, f32[256,256]{1,0:T(8,128)S(1)} %get-tuple-element.7.full_inv, bf16[256,1024]{1,0:T(8,128)(2,1)S(1)} %bitcast.3, bf16[2048,256]{1,0:T(8,128)(2,1)S(1)} %bitcast.2, bf16[2048,1024]{1,0:T(8,128)(2,1)S(1)} %copy-done), custom_call_target="tpu_custom_call" | custom-call | tf_op jit(solution)/shard_map/solve_update/pallas_call | solution.py:407
Async XLA Ops:
  0.6 27.2 %copy-start = (bf16[2048,1024]{1,0:T(8,128)(2,1)S(1)}, bf16[2048,1024]{1,0:T(8,128)(2,1)}, u32[]{:S(2)}) copy-start(bf16[2048,1024]{1,0:T(8,128)(2,1)} %trailing.3) | copy-start | bytes 12582916
